TPU v7x, 32 devices: a whole 2x2x4 slice. The times are simulated.
32 devices in a mesh: seq: 8 (over z, x), doc: 4 (over y, core).
Axes of the slice: x: 2, y: 2, z: 4, core: 2. Of those that a mesh axis runs over, the one named last changes fastest.
Arguments:
- values: bfloat16 [4, 2048, 4096], P('doc', 'seq'), may hold values from -6 to 6
- b_in: bfloat16 [4, 2048, 128], P('doc', 'seq'), may hold values from -0.032958984 to 0.032958984
- c_in: bfloat16 [4, 2048, 128], P('doc', 'seq'), may hold values from -6 to 6
- log_decay: float32 [4, 64, 2048], P('doc', None, 'seq'), may hold values from -1 to 0, as said below
- skip: float32 [64], replicated, may hold values from 0.5 to 1.5
- owner: int32 [4, 16], P(None, 'seq'), may hold values from -1 to 3, as said below
Outputs:
- owned: bfloat16 [4, 64, 128, 4096], P('doc', 'seq')
Inputs may be any that keep to these rules, and one draw needn't show every extreme that they name: `log_decay`: all entries are at most 0. In each head the per-token rates vary from token to token and from shard to shard. Within each shard of 2 blocks of a document, both blocks name the same owner (so no block is marked -1); in general -1 marks a block that is not kept.
All inputs are finite; a program needn't handle non-finite values.
Results may differ from a plain program's by a relative error of at most 0.0063.
Values may be sent and summed in bfloat16 or wider, within the bound.
A program may use at most 192 MiB of HBM per device.

v0:
```python
import jax
import jax.numpy as jnp
from jax import lax
from jax.sharding import PartitionSpec as P

Q = 128
CAP = 2


def prefix(part, axis, combine, identity):
    place = lax.axis_index(axis)
    gathered = jax.tree.map(lambda a: lax.all_gather(a, axis), part)
    state = jax.tree.map(lambda a, e: jnp.zeros_like(a) + jnp.asarray(e, a.dtype), part, identity)

    def one(step, state):
        return combine(
            state, jax.tree.map(lambda a: lax.dynamic_index_in_dim(a, step, 0, False), gathered)
        )

    return lax.fori_loop(0, place, one, state)


def block_states(value_group, b_group, cum_group):
    b_weighted = (
        b_group.astype(jnp.float32)[:, None] * jnp.exp(cum_group[:, :, -1:] - cum_group)[..., None]
    ).astype(jnp.bfloat16)
    return jnp.einsum(
        "ghsn,gshp->ghnp", b_weighted, value_group, preferred_element_type=jnp.float32
    )


def diagonal_part(value_group, b_group, c_group, cum_group, skip):
    scores = jnp.einsum("gtn,gsn->gts", c_group, b_group, preferred_element_type=jnp.float32)
    row_ids = jnp.arange(Q)
    lower_mask = (row_ids[:, None] >= row_ids[None, :])[None, None]
    decay_gap = cum_group[:, :, :, None] - cum_group[:, :, None, :]
    weights = jnp.where(
        lower_mask, scores[:, None] * jnp.exp(jnp.where(lower_mask, decay_gap, 0.0)), 0.0
    ).astype(jnp.bfloat16)
    diagonal = jnp.einsum(
        "ghts,gshp->gthp", weights, value_group, preferred_element_type=jnp.float32
    )
    return diagonal + skip[None, None, :, None] * value_group.astype(jnp.float32)


def carried_part(c_group, cum_group, enter_group):
    c_weighted = (c_group.astype(jnp.float32)[:, None] * jnp.exp(cum_group)[..., None]).astype(
        jnp.bfloat16
    )
    return jnp.einsum(
        "ghtn,ghnp->gthp", c_weighted, enter_group, preferred_element_type=jnp.float32
    )


def combine(earlier, late_pair):
    return (earlier[0] * late_pair[0], late_pair[0][:, None, None] * earlier[1] + late_pair[1])


def local(values, b_in, c_in, log_decay, skip, owner):
    seq_len = values.shape[1]
    row_width = values.shape[2]
    head_count = log_decay.shape[1]
    head_dim = row_width // head_count
    state_dim = b_in.shape[2]
    block_count = seq_len // Q
    group_size = min(4, block_count)
    round_count = block_count // group_size
    value_blocks = values[0].reshape(round_count, group_size, Q, head_count, head_dim)
    b_blocks = b_in[0].reshape(round_count, group_size, Q, state_dim)
    c_blocks = c_in[0].reshape(round_count, group_size, Q, state_dim)
    decay_rows = log_decay[0].reshape(head_count, block_count, Q).transpose(1, 0, 2)
    cum_decay = jnp.cumsum(decay_rows, axis=2)
    totals = cum_decay[:, :, -1]
    cum_groups = cum_decay.reshape(round_count, group_size, head_count, Q)

    def state_pass(inputs):
        value_group, b_group, cum_group = inputs
        return block_states(value_group, b_group, cum_group)

    states = lax.map(state_pass, (value_blocks, b_blocks, cum_groups))

    def advance(carried_in, inputs):
        block_total, block_state = inputs
        return (jnp.exp(block_total)[:, None, None] * carried_in + block_state, carried_in)

    zero_state = jnp.zeros((head_count, state_dim, head_dim), jnp.float32)
    end_state, enters = lax.scan(
        advance, zero_state, (totals, states.reshape(block_count, head_count, state_dim, head_dim))
    )
    shard_decay = jnp.exp(jnp.sum(totals, axis=0))
    carried = prefix(
        (shard_decay, end_state), "seq", combine, (jnp.ones_like(shard_decay), zero_state)
    )
    incoming = carried[1]
    before = jnp.cumsum(totals, axis=0) - totals
    enters = (enters + jnp.exp(before)[:, :, None, None] * incoming[None]).astype(jnp.bfloat16)
    enters = enters.reshape(round_count, group_size, head_count, state_dim, head_dim)

    def whole_pass(inputs):
        value_group, b_group, c_group, cum_group, enter_group = inputs
        summed = diagonal_part(value_group, b_group, c_group, cum_group, skip) + carried_part(
            c_group, cum_group, enter_group
        )
        return summed.astype(jnp.bfloat16)

    outputs = lax.map(whole_pass, (value_blocks, b_blocks, c_blocks, cum_groups, enters))
    out_blocks = outputs.reshape(block_count, Q, row_width)
    doc_count = owner.shape[0]
    owner_ids = jnp.arange(doc_count, dtype=jnp.int32)
    matches = (owner[:, None, :] == owner_ids[None, :, None]).astype(jnp.int32)
    ranking = jnp.cumsum(matches, axis=2) - 1
    slot_ids = jnp.arange(CAP, dtype=jnp.int32)
    chosen = (matches[:, :, None, :] > 0) & (
        ranking[:, :, None, :] == slot_ids[None, None, :, None]
    )
    my_doc = lax.axis_index("doc")
    list_size = min(block_count, doc_count * CAP)
    kept_mask = (owner >= 0).astype(jnp.int32)
    list_place = jnp.cumsum(kept_mask, axis=1) - 1
    spot_ids = jnp.arange(list_size, dtype=jnp.int32)
    in_list = (kept_mask[:, :, None] > 0) & (list_place[:, :, None] == spot_ids[None, None, :])
    own_list = lax.dynamic_index_in_dim(in_list, my_doc, 0, keepdims=False).astype(jnp.bfloat16)
    compact = jnp.einsum(
        "jp,jqw->pqw", own_list, out_blocks, preferred_element_type=jnp.float32
    ).astype(jnp.bfloat16)
    gathered = lax.all_gather(compact, "doc", axis=0, tiled=True).reshape(
        doc_count, list_size, Q, row_width
    )
    for_owner = lax.dynamic_index_in_dim(chosen, my_doc, 1, keepdims=False).astype(jnp.float32)
    picking = jnp.einsum("dkj,djp->dkp", for_owner, in_list.astype(jnp.float32)).astype(
        jnp.bfloat16
    )
    received = jnp.einsum(
        "dkp,dpqw->dkqw", picking, gathered, preferred_element_type=jnp.float32
    ).astype(jnp.bfloat16)
    return received.reshape(1, doc_count * CAP, Q, row_width)


def solution(mesh):
    in_specs = (
        P("doc", "seq", None),
        P("doc", "seq", None),
        P("doc", "seq", None),
        P("doc", None, "seq"),
        P(),
        P(None, "seq"),
    )
    out_specs = P("doc", "seq", None, None)
    return jax.shard_map(local, mesh=mesh, in_specs=in_specs, out_specs=out_specs, check_vma=False)
```

profile of v0, /device:TPU:25, one launch (start us, length us, event | category | flops | bytes accessed | tf_op | source)
XLA Modules:
  0.0 484.6 jit_solution(6920329098138749976)
XLA Ops:
  6.5 0.0 all-gather.7.cloned.1.call-start
  6.5 0.9 reshape_squeeze.2
  7.4 0.6 reduce_window_sum.46
  8.0 0.2 slice_reduce_fusion
  8.3 0.1 fusion.26
  8.4 6.9 %reshape.124 = bf16[2,128,64,64]{3,2,1,0:T(8,128)(2,1)} reshape(bf16[1,256,4096]{2,1,0:T(8,128)(2,1)} %param.10) | data formatting | bytes 4194304 | tf_op jit(solution)/shard_map/while/body/jit(dynamic_index_in_dim)/squeeze | solution.py:80
  15.3 5.7 %copy.53 = bf16[2,128,64,64]{1,3,2,0:T(8,128)(2,1)S(1)} copy(bf16[2,128,64,64]{3,2,1,0:T(8,128)(2,1)} %reshape.124) | data formatting | bytes 4194304 | tf_op jit(solution)/shard_map/while/body/jit(dynamic_index_in_dim)/squeeze | solution.py:80
  20.9 0.0 copy-start.1
  21.0 0.0 copy-done.3
  21.0 6.6 %fusion.4 = f32[2,64,128,64]{3,2,1,0:T(8,128)} fusion(bf16[2,128,64,64]{1,3,2,0:T(8,128)(2,1)S(1)} %copy.53, f32[2,64,128]{2,1,0:T(8,128)S(1)} %get-tuple-element.190, f32[2,128,128]{2,1,0:T(8,128)S(1)} %convert_element_type.70), kind=kOutput, calls=%fused_computation.16 | convolution fusion | flops 272629760 | bytes 6488064 | tf_op jit(solution)/shard_map/while/body/eval_jaxpr/ghsn,gshp->ghnp/dot_general | solution.py:27
  27.6 0.0 copy-done.1
  27.6 18.2 %while.7 = (s32[]{:T(128)}, f32[64,128,64]{2,1,0:T(8,128)}, f32[2,64,128,64]{3,2,1,0:T(8,128)}, f32[2,64]{1,0:T(2,128)S(1)}, f32[2,64,128,64]{3,2,1,0:T(8,128)}, /*index=5*/s32[]{:T(128)}, s32[]{:T(128)}) while((s32[]{:T(128)}, f32[64,128,64]{2,1,0:T(8,128)}, f32[2,64,128,64]{3,2,1,0:T(8,128)}, f32[2,64]{1,0:T(2,128)S(1)}, ...), condition=%wide.region_4.5_spmd.clone, body=%wide.region_3.4_spmd.clone.sunk | while | flops 2097155 | bytes 31458680 | solution.py:87
  27.6 2.7 bitcast_dynamic-update-slice_fusion.2
  30.3 2.2 copy-done
  32.5 2.5 bitcast_add_fusion.7
  35.0 5.0 %bitcast_dynamic-update-slice_fusion.2 = f32[2,64,128,64]{3,2,1,0:T(8,128)} fusion(f32[2,64,128,64]{3,2,1,0:T(8,128)} %get-tuple-element.267, s32[]{:T(128)} %get-tuple-element.265, f32[64,128,64]{2,1,0:T(8,128)} %get-tuple-element.266, pred[]{:T(512)S(6)} %compare.3), kind=kLoop, calls=%fused_computation.3.clone.1 | loop fusion | flops 524288 | bytes 8389121 | tf_op jit(solution)/shard_map/while/body/jit(dynamic_update_index_in_dim)/dynamic_update_slice | solution.py:87
  40.0 1.1 copy-done
  41.2 4.7 bitcast_add_fusion.7
  45.8 3.9 copy.57
  49.7 0.0 all-gather.7.cloned.1.call-update
  49.7 0.0 all-gather.5.cloned.1.call-start
  49.8 0.0 copy-done.7
  49.8 0.6 dynamic-slice.2
  50.9 0.1 exponential_dynamic-update-slice_fusion
  51.1 13.7 %all-reduce = f32[512]{0:T(512)S(1)} all-reduce(f32[512]{0:T(512)S(1)} %exponential_dynamic-update-slice_fusion), channel_id=2, replica_groups=mesh['seq'=8,'doc'=4] {'seq'}, use_global_device_ids=true, to_apply=%add | all-reduce | flops 512 | bytes 4096
  64.8 0.1 reshape.115
  65.0 0.1 copy.49
  65.1 0.1 copy.48
  65.2 0.1 compare_and_fusion
  65.3 0.2 fusion.27
  65.4 211.5 %all-gather.7.cloned.1.call-done = f32[512,128,64]{1,2,0:T(8,128)} async-done(((f32[64,128,64]{1,2,0:T(8,128)}), f32[512,128,64]{1,2,0:T(8,128)}) %all-gather.7.cloned.1.call-update) | async-done | bytes 16777232 | tf_op jit(solution)/shard_map/all_gather | solution.py:12
  276.9 2.4 broadcast_in_dim.78
  279.3 62.0 %while.6 = (s32[]{:T(128)}, f32[64,128,64]{2,1,0:T(8,128)}, s32[]{:T(128)}, f32[8,64]{1,0:T(8,128)S(1)}, f32[8,64,128,64]{2,3,1,0:T(8,128)}, /*index=5*/s32[]{:T(128)}, s32[]{:T(128)}, s32[]{:T(128)}) while((s32[]{:T(128)}, f32[64,128,64]{2,1,0:T(8,128)}, s32[]{:T(128)}, f32[8,64]{1,0:T(8,128)S(1)}, f32[8,64,128,64]{2,3,1,0:T(8,128)}, ...), condition=%wide.region_8.9_spmd, body=%wide.region_7.8_spmd.sunk | while | flops 1048581 | bytes 14680959 | solution.py:20
  279.3 1.7 constant_dynamic-slice_fusion.5
  281.1 2.7 copy.81
  283.8 5.9 %bitcast_add_fusion.6 = f32[64,128,64]{2,1,0:T(8,128)} fusion(f32[1,64,128,64]{3,2,1,0:T(8,128)} %copy.81, f32[64,128,64]{2,1,0:T(8,128)} %get-tuple-element.288, f32[64]{0:T(128)S(1)} %dynamic-slice_bitcast_fusion.4), kind=kLoop, calls=%fused_computation.clone.1 | loop fusion | flops 1048576 | bytes 6291712 | tf_op jit(solution)/shard_map/while/body/add | solution.py:56
  289.7 1.7 constant_dynamic-slice_fusion.5
  291.4 2.7 copy.81
  294.1 5.9 %bitcast_add_fusion.6 = f32[64,128,64]{2,1,0:T(8,128)} fusion(f32[1,64,128,64]{3,2,1,0:T(8,128)} %copy.81, f32[64,128,64]{2,1,0:T(8,128)} %get-tuple-element.288, f32[64]{0:T(128)S(1)} %dynamic-slice_bitcast_fusion.4), kind=kLoop, calls=%fused_computation.clone.1 | loop fusion | flops 1048576 | bytes 6291712 | tf_op jit(solution)/shard_map/while/body/add | solution.py:56
  300.0 1.7 constant_dynamic-slice_fusion.5
  301.7 2.7 copy.81
  304.5 5.9 %bitcast_add_fusion.6 = f32[64,128,64]{2,1,0:T(8,128)} fusion(f32[1,64,128,64]{3,2,1,0:T(8,128)} %copy.81, f32[64,128,64]{2,1,0:T(8,128)} %get-tuple-element.288, f32[64]{0:T(128)S(1)} %dynamic-slice_bitcast_fusion.4), kind=kLoop, calls=%fused_computation.clone.1 | loop fusion | flops 1048576 | bytes 6291712 | tf_op jit(solution)/shard_map/while/body/add | solution.py:56
  310.3 1.7 constant_dynamic-slice_fusion.5
  312.1 2.7 copy.81
  314.8 5.9 %bitcast_add_fusion.6 = f32[64,128,64]{2,1,0:T(8,128)} fusion(f32[1,64,128,64]{3,2,1,0:T(8,128)} %copy.81, f32[64,128,64]{2,1,0:T(8,128)} %get-tuple-element.288, f32[64]{0:T(128)S(1)} %dynamic-slice_bitcast_fusion.4), kind=kLoop, calls=%fused_computation.clone.1 | loop fusion | flops 1048576 | bytes 6291712 | tf_op jit(solution)/shard_map/while/body/add | solution.py:56
  320.7 1.7 constant_dynamic-slice_fusion.5
  322.4 2.7 copy.81
  325.2 5.9 %bitcast_add_fusion.6 = f32[64,128,64]{2,1,0:T(8,128)} fusion(f32[1,64,128,64]{3,2,1,0:T(8,128)} %copy.81, f32[64,128,64]{2,1,0:T(8,128)} %get-tuple-element.288, f32[64]{0:T(128)S(1)} %dynamic-slice_bitcast_fusion.4), kind=kLoop, calls=%fused_computation.clone.1 | loop fusion | flops 1048576 | bytes 6291712 | tf_op jit(solution)/shard_map/while/body/add | solution.py:56
  331.0 1.7 constant_dynamic-slice_fusion.5
  332.7 2.7 copy.81
  335.5 5.9 %bitcast_add_fusion.6 = f32[64,128,64]{2,1,0:T(8,128)} fusion(f32[1,64,128,64]{3,2,1,0:T(8,128)} %copy.81, f32[64,128,64]{2,1,0:T(8,128)} %get-tuple-element.288, f32[64]{0:T(128)S(1)} %dynamic-slice_bitcast_fusion.4), kind=kLoop, calls=%fused_computation.clone.1 | loop fusion | flops 1048576 | bytes 6291712 | tf_op jit(solution)/shard_map/while/body/add | solution.py:56
  341.3 8.0 %fusion.5 = f32[2,64,64,128]{3,2,1,0:T(8,128)S(1)} fusion(f32[2,64,128,64]{3,2,1,0:T(8,128)} %get-tuple-element.116, f32[2,64,128]{2,1,0:T(8,128)S(1)} %get-tuple-element.189, f32[2,128,128]{2,1,0:T(8,128)S(1)} %convert_element_type.73, f32[64,128,64]{2,1,0:T(8,128)} %get-tuple-element.118, f32[2,64]{1,0:T(2,128)S(1)} %subtract_exponential_fusion.1), kind=kOutput, calls=%fused_computation.17 | convolution fusion | flops 275775488 | bytes 10682880 | tf_op jit(solution)/shard_map/while/body/eval_jaxpr/ghtn,ghnp->gthp/dot_general | solution.py:50
  349.3 0.0 copy-done.2
  349.3 0.0 copy-done.6
  349.3 4.8 fusion.6
  354.2 3.8 copy.61
  358.0 4.7 convolution_convert_fusion.1
  362.7 2.6 copy.62
  365.3 0.0 all-gather.5.cloned.1.call-update
  365.4 0.1 copy.47
  365.5 0.7 reduce_window_sum.44
  366.2 68.2 %all-gather.5.cloned.1.call-done = bf16[8,128,4096]{2,1,0:T(8,128)(2,1)} async-done(((bf16[2,128,4096]{2,1,0:T(8,128)(2,1)}), bf16[8,128,4096]{2,1,0:T(8,128)(2,1)}) %all-gather.5.cloned.1.call-update) | async-done | bytes 8388624 | tf_op jit(solution)/shard_map/all_gather | solution.py:126
  434.3 30.6 %convolution_convert_fusion = bf16[4,2,128,4096]{3,1,2,0:T(2,128)(2,1)} fusion(bf16[4,2,128,4096]{3,2,1,0:T(8,128)(2,1)} %bitcast.64, pred[4,2,2]{2,1,0:T(4,128)(4,1)S(1)} %compare_and_fusion, pred[4,2,2]{2,0,1:T(4,128)(4,1)S(1)} %fusion.23), kind=kOutput, calls=%fused_computation.8 | convolution fusion | flops 20971600 | bytes 16777248 | tf_op jit(solution)/shard_map/dkp,dpqw->dkqw/dot_general | solution.py:133
  464.9 12.8 %copy.64 = bf16[4,2,128,4096]{3,2,1,0:T(8,128)(2,1)} copy(bf16[4,2,128,4096]{3,1,2,0:T(2,128)(2,1)} %convolution_convert_fusion) | data formatting | bytes 16777216 | tf_op jit(solution)/shard_map/convert_element_type | solution.py:135
  (35 shorter events, 0.2 us)
Async XLA Ops:
  6.5 270.4 %all-gather.7.cloned.1.call-start = ((), (), s32[]{:S(2)}) async-start(), calls=%async_computation.1 | async-start | bytes 18874368 | tf_op jit(solution)/shard_map/all_gather | solution.py:12
  15.3 5.7 %copy-start.3 = (bf16[1,256,128]{2,1,0:T(8,128)(2,1)S(1)}, bf16[1,256,128]{2,1,0:T(8,128)(2,1)}, u32[]{:S(2)}) copy-start(bf16[1,256,128]{2,1,0:T(8,128)(2,1)} %param.11) | copy-start | bytes 196612
  20.9 6.7 %copy-start.1 = (bf16[2,128,64,64]{1,3,2,0:T(8,128)(2,1)}, bf16[2,128,64,64]{1,3,2,0:T(8,128)(2,1)S(1)}, u32[]{:S(2)}) copy-start(bf16[2,128,64,64]{1,3,2,0:T(8,128)(2,1)S(1)} %copy.53) | copy-start | bytes 6291460
  27.6 4.9 %copy-start = (f32[2,64,128,64]{3,2,1,0:T(8,128)S(1)}, f32[2,64,128,64]{3,2,1,0:T(8,128)}, u32[]{:S(2)}) copy-start(f32[2,64,128,64]{3,2,1,0:T(8,128)} %get-tuple-element.276) | copy-start | bytes 12582916 | tf_op jit(solution)/shard_map/while
  35.0 6.2 %copy-start = (f32[2,64,128,64]{3,2,1,0:T(8,128)S(1)}, f32[2,64,128,64]{3,2,1,0:T(8,128)}, u32[]{:S(2)}) copy-start(f32[2,64,128,64]{3,2,1,0:T(8,128)} %get-tuple-element.276) | copy-start | bytes 12582916 | tf_op jit(solution)/shard_map/while
  45.8 4.0 copy-start.7
  45.8 19.0 %copy-start.4 = (bf16[1,256,128]{2,1,0:T(8,128)(2,1)S(1)}, bf16[1,256,128]{2,1,0:T(8,128)(2,1)}, u32[]{:S(2)}) copy-start(bf16[1,256,128]{2,1,0:T(8,128)(2,1)} %param.12) | copy-start | bytes 196612
  45.8 19.1 %copy-start.5 = (s32[4,2]{0,1:T(2,128)S(1)}, s32[4,2]{0,1:T(2,128)}, u32[]{:S(2)}) copy-start(s32[4,2]{0,1:T(2,128)} %param.15) | copy-start | bytes 100
  49.7 384.6 %all-gather.5.cloned.1.call-start = ((), (), s32[]{:S(2)}) async-start(), calls=%async_computation | async-start | bytes 10485760 | tf_op jit(solution)/shard_map/all_gather | solution.py:126
  341.3 8.0 %copy-start.2 = (bf16[2,128,64,64]{1,3,2,0:T(8,128)(2,1)S(1)}, bf16[2,128,64,64]{1,3,2,0:T(8,128)(2,1)}, u32[]{:S(2)}) copy-start(bf16[2,128,64,64]{1,3,2,0:T(8,128)(2,1)} %copy-done.1) | copy-start | bytes 6291460
  341.3 8.0 %copy-start.6 = (f32[64]{0:T(128)S(1)}, f32[64]{0:T(128)}, u32[]{:S(2)}) copy-start(f32[64]{0:T(128)} %param.14) | copy-start | bytes 772
Sparse Core Ops, SparseCore 0:
  49.9 226.9 all-gather.6
  365.5 68.8 all-gather.4
where the time goes:
time: 487 us; the launch traced here: 485 us
  waiting for transfers between devices  280 us (57%)
  local copies, waits for them, and re-layouts  70.2 us (14%)
  matrix products  54.9 us (11%)
  other arithmetic  51.8 us (11%)
  between operations  14.1 us (3%)
  blocking collectives  13.7 us (3%)
    all_gather x1, waiting for transfers between devices, prefix(): gathered = jax.tree.map(lambda a: lax.all_gather(a, axis), part)  211 us
    all_gather x1, waiting for transfers between devices, local(): lax.all_gather(compact, 'doc', axis=0, tiled=True)  68.2 us
    add x6, other arithmetic, combine(): late_pair[0][:, None, None] * earlier[1] + late_pair[1]  35.2 us
    dot_general x1, matrix products, local(): jnp.einsum('dkp,dpqw->dkqw', picking, gathered, preferred_element_type=jn...  30.6 us
    dynamic_slice x12, local copies, waits for them, and re-layouts, one(): lax.dynamic_index_in_dim(a, step, 0, False)  26.8 us
    unnamed x1, blocking collectives  13.7 us
    convert_element_type x1, local copies, waits for them, and re-layouts, local(): received = jnp.einsum('dkp,dpqw->dkqw', picking, gathered, preferred_elem...  12.8 us
    squeeze x2, local copies, waits for them, and re-layouts, local(): states = lax.map(state_pass, (value_blocks, b_blocks, cum_groups))  12.6 us
  transfers between devices with their start and end apart: 2, of which 2 were waited for; matrix products, arithmetic and copies ran while one was open for 0% of the time, Pallas kernels for 0%

commit v1 on v0

v1 whole, which is shorter than its diff:
```python
import functools

import jax
import jax.numpy as jnp
from jax import lax
from jax.experimental import pallas as pl
from jax.experimental.pallas import tpu as pltpu
from jax.sharding import PartitionSpec as P

Q = 128
CAP = 2
MESH = pl.DeviceIdType.MESH
F32 = jnp.float32
BF16 = jnp.bfloat16


def layer_kernel(
    n_seq, n_doc, heads, width, chunks,
    v_hbm, b_ref, c_ref, ld_ref, skip_ref, gathered,
    v_buf, lhs_buf, sb_buf, a_buf, d_buf, row_buf, l_buf, x_out, x_in, z_out, z_in, o_buf,
    v_sem, own_sem, xs, xr, zs, zr, ys, yr, cs, cr, fs, fr,
):
    seq_len, row_width = v_buf.shape
    blocks = seq_len // Q
    state_dim = b_ref.shape[1]
    head_dim = row_width // heads
    sides = n_doc // 2
    rungs = n_seq // 2
    seq = lax.axis_index("seq")
    doc = lax.axis_index("doc")
    rung, second = seq // 2, seq % 2
    side, core = doc // 2, doc % 2
    across = (seq + 1 - 2 * second, doc)
    above = (seq + 2, doc)
    below = (seq - 2, doc)
    twin = (seq, doc + 1 - 2 * core)
    far = [(seq, ((side + j) % sides) * 2 + core) for j in range(1, sides)]

    load = pltpu.make_async_copy(v_hbm, v_buf, v_sem)
    load.start()

    barrier = pltpu.get_barrier_semaphore()
    for other in [across, twin] + far:
        pl.semaphore_signal(barrier, inc=1, device_id=other, device_id_type=MESH)

    @pl.when(rung > 0)
    def _():
        pl.semaphore_signal(barrier, inc=1, device_id=below, device_id_type=MESH)

    @pl.when(rung < rungs - 1)
    def _():
        pl.semaphore_signal(barrier, inc=1, device_id=above, device_id_type=MESH)

    rows_i = lax.broadcasted_iota(jnp.int32, (Q, Q), 0)
    cols_i = lax.broadcasted_iota(jnp.int32, (Q, Q), 1)
    lower = rows_i >= cols_i
    ones_lower = jnp.where(lower, 1.0, 0.0).astype(F32)
    lane = lax.broadcasted_iota(jnp.int32, (1, 2 * heads), 1)
    twice = (
        lax.broadcasted_iota(jnp.int32, (heads, 2 * heads), 1) % heads
        == lax.broadcasted_iota(jnp.int32, (heads, 2 * heads), 0)
    )
    skip_row = jnp.dot(
        jnp.broadcast_to(skip_ref[...], (8, heads)), jnp.where(twice, 1.0, 0.0).astype(F32),
        precision=lax.Precision.HIGHEST, preferred_element_type=F32,
    )[0:1]

    def split(x):
        high = x.astype(BF16).astype(F32)
        return jnp.where(lane < heads, high, x - high).astype(BF16)

    small = [skip_row]
    halves, totals, befores = [], [], []
    running = jnp.zeros((1, 2 * heads), F32)
    for k in range(blocks):
        span = slice(k * Q, (k + 1) * Q)
        decay = ld_ref[:, span]
        decay = jnp.concatenate([decay, decay], axis=0)
        cum = lax.dot_general(
            ones_lower, decay, (((1,), (1,)), ((), ())),
            precision=lax.Precision.HIGHEST, preferred_element_type=F32,
        )
        total = cum[Q - 1:Q]
        half = 0.5 * total
        lhs_buf[2 * k * Q:(2 * k + 1) * Q, :] = split(jnp.exp(cum - half))
        lhs_buf[(2 * k + 1) * Q:(2 * k + 2) * Q, :] = split(jnp.exp(half - cum))
        running = running + total
        halves.append(jnp.exp(half))
        totals.append(jnp.exp(total))
        befores.append(jnp.exp(running))
        b_block = b_ref[span, :]
        scores = lax.dot_general(
            c_ref[span, :], b_block, (((1,), (1,)), ((), ())), preferred_element_type=F32
        )
        sb_buf[k, 0:Q, :] = jnp.where(lower, scores, 0.0).astype(BF16)
        sb_buf[k, Q:Q + state_dim, :] = b_block.astype(F32).T.astype(BF16)
    small = [skip_row] + halves + totals + befores
    row_count = row_buf.shape[1]
    row_id = lax.broadcasted_iota(jnp.int32, (row_count, 2 * heads), 0)
    stacked = jnp.zeros((row_count, 2 * heads), F32)
    for i, row in enumerate(small):
        stacked = jnp.where(row_id == i, row, stacked)
    base = 2 * blocks * Q
    lhs_buf[base:base + row_count, :] = split(stacked)

    @pl.when(rung == 0)
    def _():
        z_in[...] = jnp.zeros_like(z_in)

    peers = 2 + len(far) + jnp.where(rung > 0, 1, 0) + jnp.where(rung < rungs - 1, 1, 0)
    pl.semaphore_wait(barrier, peers)
    load.wait()

    def x_copy(g):
        return pltpu.make_async_remote_copy(
            x_out.at[g], x_in.at[g], xs.at[g], xr.at[g], device_id=across, device_id_type=MESH)

    def z_copy(g):
        return pltpu.make_async_remote_copy(
            z_out.at[g], z_in.at[g], zs.at[g], zr.at[g], device_id=above, device_id_type=MESH)

    def far_copy(j, g):
        return pltpu.make_async_remote_copy(
            o_buf.at[g], gathered.at[doc, g], ys.at[j, g], yr.at[j, g],
            device_id=far[j], device_id_type=MESH)

    def twin_copy(g):
        return pltpu.make_async_remote_copy(
            o_buf.at[g], gathered.at[doc, g], cs.at[g], cr.at[g],
            device_id=twin, device_id_type=MESH)

    def own_copy(g):
        return pltpu.make_async_copy(o_buf.at[g], gathered.at[doc, g], own_sem.at[g])

    def forward_copy(j, g):
        source = ((side + sides - 1 - j) % sides) * 2 + core
        return pltpu.make_async_remote_copy(
            gathered.at[source, g], gathered.at[source, g], fs.at[j, g], fr.at[j, g],
            device_id=twin, device_id_type=MESH)

    def local_part(g, carry):
        lanes = pl.ds(pl.multiple_of(g * width, width), width)
        head_of = lax.broadcasted_iota(jnp.int32, (2 * heads, width), 1) // head_dim
        head_at = lax.broadcasted_iota(jnp.int32, (2 * heads, width), 0) % heads
        spread = jnp.where(head_at == head_of + g * (width // head_dim), 1.0, 0.0).astype(BF16)
        rows = jnp.dot(lhs_buf[base:base + row_count, :], spread, preferred_element_type=F32)
        row_buf[g] = rows
        state = jnp.zeros((state_dim, width), F32)
        for k in range(blocks):
            a_buf[g, k * Q:(k + 1) * Q, :] = jnp.dot(
                lhs_buf[2 * k * Q:(2 * k + 1) * Q, :], spread, preferred_element_type=F32)
            grow = jnp.dot(
                lhs_buf[(2 * k + 1) * Q:(2 * k + 2) * Q, :], spread, preferred_element_type=F32)
            scaled = (v_buf[k * Q:(k + 1) * Q, lanes].astype(F32) * grow).astype(BF16)
            both = jnp.dot(sb_buf[k], scaled, preferred_element_type=F32)
            d_buf[g, k * Q:(k + 1) * Q, :] = both[0:Q]
            state = rows[1 + blocks + k:2 + blocks + k] * state + rows[1 + k:2 + k] * both[Q:]
            l_buf[k, g] = state
        x_out[g, 0:state_dim, :] = state.astype(BF16)
        decay = rows[3 * blocks:3 * blocks + 1]
        high = decay.astype(BF16).astype(F32)
        tail = lax.broadcasted_iota(jnp.int32, (16, width), 0)
        x_out[g, state_dim:state_dim + 16, :] = jnp.where(
            tail == 0, high, jnp.where(tail == 1, decay - high, 0.0)).astype(BF16)
        x_copy(g).start()
        return carry

    lax.fori_loop(0, chunks, local_part, 0)

    def carried_part(g, carry):
        lanes = pl.ds(pl.multiple_of(g * width, width), width)
        rows = row_buf[g]
        x_copy(g).wait_recv()
        other = x_in[g, 0:state_dim, :].astype(F32)
        other_tail = x_in[g, state_dim:state_dim + 16, :].astype(F32)
        other_decay = other_tail[0:1] + other_tail[1:2]
        mine = l_buf[blocks - 1, g]
        mine_decay = rows[3 * blocks:3 * blocks + 1]
        is_second = second == 1
        first_state = jnp.where(is_second, other, mine)
        last_state = jnp.where(is_second, mine, other)
        first_decay = jnp.where(is_second, other_decay, mine_decay)
        last_decay = jnp.where(is_second, mine_decay, other_decay)

        @pl.when(rung > 0)
        def _():
            z_copy(g).wait_recv()

        enter = z_in[g].astype(F32)
        middle = first_decay * enter + first_state

        @pl.when(rung < rungs - 1)
        def _():
            z_out[g] = (last_decay * middle + last_state).astype(BF16)
            z_copy(g).start()

        enter = jnp.where(is_second, middle, enter)
        skip_lanes = rows[0:1]
        for k in range(blocks):
            span = slice(k * Q, (k + 1) * Q)
            at_block = enter
            if k > 0:
                at_block = rows[2 * blocks + k:2 * blocks + k + 1] * enter + l_buf[k - 1, g]
            scaled = (rows[1 + k:2 + k] * at_block).astype(BF16)
            inner = d_buf[g, span, :] + jnp.dot(
                c_ref[span, :], scaled, preferred_element_type=F32)
            o_buf[g, span, :] = (
                a_buf[g, span, :] * inner + skip_lanes * v_buf[span, lanes].astype(F32)
            ).astype(BF16)
        for j in range(len(far)):
            far_copy(j, g).start()
        twin_copy(g).start()
        own_copy(g).start()
        return carry

    lax.fori_loop(0, chunks, carried_part, 0)

    def forward(g, carry):
        for j in range(len(far)):
            far_copy(j, g).wait_recv()
            forward_copy(j, g).start()
        return carry

    lax.fori_loop(0, chunks, forward, 0)

    def finish(g, carry):
        x_copy(g).wait_send()

        @pl.when(rung < rungs - 1)
        def _():
            z_copy(g).wait_send()

        for j in range(len(far)):
            far_copy(j, g).wait_send()
            forward_copy(j, g).wait()
        twin_copy(g).wait()
        own_copy(g).wait()
        return carry

    lax.fori_loop(0, chunks, finish, 0)


def slot_source(index, owner, me, blocks):
    doc, rank = index // CAP, index % CAP
    seen = jnp.int32(0)
    block = jnp.int32(0)
    present = jnp.bool_(False)
    for j in range(blocks):
        match = owner[doc * blocks + j] == me
        hit = match & (seen == rank)
        block = jnp.where(hit, j, block)
        present = present | hit
        seen = seen + match.astype(jnp.int32)
    return present, doc, block


def pick_kernel(blocks, owner, me, taken, out):
    present, _, _ = slot_source(pl.program_id(0), owner, me[0], blocks)
    chunks, width = taken.shape[1], taken.shape[3]

    @pl.when(present)
    def _():
        for g in range(chunks):
            out[0, 0, :, g * width:(g + 1) * width] = taken[0, g]

    @pl.when(jnp.logical_not(present))
    def _():
        out[...] = jnp.zeros_like(out)


def local(n_seq, n_doc, values, b_in, c_in, log_decay, skip, owner):
    seq_len, row_width = values.shape[1], values.shape[2]
    heads = log_decay.shape[1]
    state_dim = b_in.shape[2]
    blocks = seq_len // Q
    width = min(256, row_width)
    chunks = row_width // width
    far = n_doc // 2 - 1
    row_count = -(-(1 + 3 * blocks) // 16) * 16
    vmem = pl.BlockSpec(memory_space=pltpu.VMEM)
    anywhere = pl.BlockSpec(memory_space=pl.ANY)
    dma = pltpu.SemaphoreType.DMA
    gathered = pl.pallas_call(
        functools.partial(layer_kernel, n_seq, n_doc, heads, width, chunks),
        out_shape=jax.ShapeDtypeStruct((n_doc, chunks, seq_len, width), BF16),
        in_specs=[anywhere, vmem, vmem, vmem, vmem],
        out_specs=anywhere,
        scratch_shapes=[
            pltpu.VMEM((seq_len, row_width), BF16),
            pltpu.VMEM((2 * seq_len + row_count, 2 * heads), BF16),
            pltpu.VMEM((blocks, Q + state_dim, Q), BF16),
            pltpu.VMEM((chunks, seq_len, width), F32),
            pltpu.VMEM((chunks, seq_len, width), F32),
            pltpu.VMEM((chunks, row_count, width), F32),
            pltpu.VMEM((blocks, chunks, state_dim, width), F32),
            pltpu.VMEM((chunks, state_dim + 16, width), BF16),
            pltpu.VMEM((chunks, state_dim + 16, width), BF16),
            pltpu.VMEM((chunks, state_dim, width), BF16),
            pltpu.VMEM((chunks, state_dim, width), BF16),
            pltpu.VMEM((chunks, seq_len, width), BF16),
            dma(()),
            dma((chunks,)),
            dma((chunks,)),
            dma((chunks,)),
            dma((chunks,)),
            dma((chunks,)),
            dma((far, chunks)),
            dma((far, chunks)),
            dma((chunks,)),
            dma((chunks,)),
            dma((far, chunks)),
            dma((far, chunks)),
        ],
        compiler_params=pltpu.CompilerParams(
            collective_id=0, has_side_effects=True, vmem_limit_bytes=44 * 2**20
        ),
        name="layer",
    )(values[0], b_in[0], c_in[0], log_decay[0], skip.reshape(1, heads))

    slots = n_doc * CAP
    me = lax.axis_index("doc").astype(jnp.int32).reshape(1)

    def taken_at(i, owner, me):
        doc_at, block_at = jnp.int32(0), jnp.int32(0)
        for j in range(slots):
            present, doc, block = slot_source(j, owner, me[0], blocks)
            use = present & (j <= i)
            doc_at = jnp.where(use, doc, doc_at)
            block_at = jnp.where(use, block, block_at)
        return doc_at, 0, block_at, 0

    return pl.pallas_call(
        functools.partial(pick_kernel, blocks),
        out_shape=jax.ShapeDtypeStruct((1, slots, Q, row_width), BF16),
        grid_spec=pltpu.PrefetchScalarGridSpec(
            num_scalar_prefetch=2,
            grid=(slots,),
            in_specs=[pl.BlockSpec((1, chunks, Q, width), taken_at)],
            out_specs=pl.BlockSpec((1, 1, Q, row_width), lambda i, owner, me: (0, i, 0, 0)),
        ),
        compiler_params=pltpu.CompilerParams(vmem_limit_bytes=16 * 2**20),
        name="pick",
    )(owner.reshape(-1), me, gathered)


def solution(mesh):
    in_specs = (
        P("doc", "seq", None),
        P("doc", "seq", None),
        P("doc", "seq", None),
        P("doc", None, "seq"),
        P(),
        P(None, "seq"),
    )
    out_specs = P("doc", "seq", None, None)
    body = functools.partial(local, mesh.shape["seq"], mesh.shape["doc"])
    return jax.shard_map(body, mesh=mesh, in_specs=in_specs, out_specs=out_specs, check_vma=False)
```

time: 487 us -> 83.6 us (0.17)
  waiting for transfers between devices: 280 us -> 0 us
  Pallas kernels: 0 us -> 74.2 us
  local copies, waits for them, and re-layouts: 70.2 us -> 8.99 us
  matrix products: 54.9 us -> 0 us
  other arithmetic: 51.8 us -> 0 us
  between operations: 14.1 us -> 0.02 us
  blocking collectives: 13.7 us -> 0 us
    all_gather x2 -> x0, waiting for transfers between devices: 280 us -> none  [the longest x1 211 us: prefix(): gathered = jax.tree.map(lambda a: lax.all_gather(a, axis), part)]
    pallas_call x0 -> x2, Pallas kernels: none -> 74.2 us  [the longest x1 68.8 us: local(): pl.pallas_call(functools.partial(layer_kernel, n_seq, n_doc, heads, width...]
    dot_general x6 -> x0, matrix products: 54.9 us -> none  [the longest x1 30.6 us: local(): jnp.einsum('dkp,dpqw->dkqw', picking, gathered, preferred_element_type=jn...]
    add x8 -> x0, other arithmetic: 42.3 us -> none  [the longest x6 35.2 us: combine(): late_pair[0][:, None, None] * earlier[1] + late_pair[1]]
    dynamic_slice x14 -> x0, local copies, waits for them, and re-layouts: 26.8 us -> none  [the longest x12 26.8 us: one(): lax.dynamic_index_in_dim(a, step, 0, False)]
    convert_element_type x2 -> x0, local copies, waits for them, and re-layouts: 15.4 us -> none  [the longest x1 12.8 us: local(): received = jnp.einsum('dkp,dpqw->dkqw', picking, gathered, preferred_elem...]
    unnamed x1 -> x0, blocking collectives: 13.7 us -> none
    squeeze x2 -> x0, local copies, waits for them, and re-layouts: 12.6 us -> none  [local(): states = lax.map(state_pass, (value_blocks, b_blocks, cum_groups))]
  transfers between devices with their start and end apart: 2 -> 0, of which waited for: 2 -> 0; matrix products, arithmetic and copies ran while one was open for 0% -> 0% of each run, Pallas kernels for 0% -> 0%
where the time goes in v1:
time: 83.6 us; the launch traced here: 83.2 us
  Pallas kernels  74.2 us (89%)
  local copies, waits for them, and re-layouts  8.99 us (11%)
    pallas_call x1, Pallas kernels, local(): pl.pallas_call(functools.partial(layer_kernel, n_seq, n_doc, heads, width...  68.8 us
    unnamed x13, local copies, waits for them, and re-layouts  8.9 us
    pallas_call x1, Pallas kernels, local(): pl.pallas_call(functools.partial(pick_kernel, blocks), out_shape=jax.Shap...  5.41 us

profile of v1, /device:TPU:25, one launch (start us, length us, event | category | flops | bytes accessed | tf_op | source)
XLA Modules:
  0.0 83.2 jit_solution(16603523001367085807)
XLA Ops:
  0.0 0.8 copy.8
  0.8 0.1 reshape.9.owner
  0.9 0.0 copy-start.1
  0.9 1.6 %copy-done.1 = bf16[1,256,4096]{2,1,0:T(8,128)(2,1)S(1)} copy-done((bf16[1,256,4096]{2,1,0:T(8,128)(2,1)S(1)}, bf16[1,256,4096]{2,1,0:T(8,128)(2,1)}, u32[]{:S(2)}) %copy-start.1) | copy-done | bytes 2097176
  2.4 0.0 copy-start.2
  2.4 0.8 %copy-done.2 = bf16[1,256,128]{2,1,0:T(8,128)(2,1)S(1)} copy-done((bf16[1,256,128]{2,1,0:T(8,128)(2,1)S(1)}, bf16[1,256,128]{2,1,0:T(8,128)(2,1)}, u32[]{:S(2)}) %copy-start.2) | copy-done | bytes 65560
  3.3 0.0 copy-start.3
  3.3 0.8 %copy-done.3 = bf16[1,256,128]{2,1,0:T(8,128)(2,1)S(1)} copy-done((bf16[1,256,128]{2,1,0:T(8,128)(2,1)S(1)}, bf16[1,256,128]{2,1,0:T(8,128)(2,1)}, u32[]{:S(2)}) %copy-start.3) | copy-done | bytes 65560
  4.1 0.0 copy-start.4
  4.1 0.8 %copy-done.4 = f32[1,64,256]{2,1,0:T(8,128)S(1)} copy-done((f32[1,64,256]{2,1,0:T(8,128)S(1)}, f32[1,64,256]{2,1,0:T(8,128)}, u32[]{:S(2)}) %copy-start.4) | copy-done | bytes 65560
  5.0 0.0 copy-start.5
  5.0 0.7 copy-done.5
  5.6 68.8 %layer.1.taken = bf16[4,16,256,256]{3,2,1,0:T(8,128)(2,1)} custom-call(bf16[256,4096]{1,0:T(8,128)(2,1)S(1)} %bitcast.6, bf16[256,128]{1,0:T(8,128)(2,1)S(1)} %bitcast.7, bf16[256,128]{1,0:T(8,128)(2,1)S(1)} %bitcast.8, f32[64,256]{1,0:T(8,128)S(1)} %bitcast.9, f32[1,64]{1,0:T(1,128)S(1)} %bitcast.10), custom_call_target="tpu_custom_call" | custom-call | tf_op jit(solution)/shard_map/layer/pallas_call | solution.py:283
  74.5 0.0 copy-start
  74.5 3.4 %copy-done = bf16[4,16,256,256]{3,2,1,0:T(8,128)(2,1)S(1)} copy-done((bf16[4,16,256,256]{3,2,1,0:T(8,128)(2,1)S(1)}, bf16[4,16,256,256]{3,2,1,0:T(8,128)(2,1)}, u32[]{:S(2)}) %copy-start) | copy-done | bytes 8388632
  77.8 5.4 %pick.1 = bf16[1,8,128,4096]{3,2,1,0:T(8,128)(2,1)} custom-call(s32[8]{0:T(128)S(1)} %reshape.9.owner, s32[1]{0:T(128)} %bitcast.me, bf16[4,16,256,256]{3,2,1,0:T(8,128)(2,1)S(1)} %copy-done), custom_call_target="tpu_custom_call" | custom-call | tf_op jit(solution)/shard_map/pick/pallas_call | solution.py:332
Async XLA Ops:
  0.9 1.6 %copy-start.1 = (bf16[1,256,4096]{2,1,0:T(8,128)(2,1)S(1)}, bf16[1,256,4096]{2,1,0:T(8,128)(2,1)}, u32[]{:S(2)}) copy-start(bf16[1,256,4096]{2,1,0:T(8,128)(2,1)} %param.6) | copy-start | bytes 6291460
  2.4 0.8 %copy-start.2 = (bf16[1,256,128]{2,1,0:T(8,128)(2,1)S(1)}, bf16[1,256,128]{2,1,0:T(8,128)(2,1)}, u32[]{:S(2)}) copy-start(bf16[1,256,128]{2,1,0:T(8,128)(2,1)} %param.7) | copy-start | bytes 196612
  3.3 0.8 %copy-start.3 = (bf16[1,256,128]{2,1,0:T(8,128)(2,1)S(1)}, bf16[1,256,128]{2,1,0:T(8,128)(2,1)}, u32[]{:S(2)}) copy-start(bf16[1,256,128]{2,1,0:T(8,128)(2,1)} %param.8) | copy-start | bytes 196612
  4.1 0.8 %copy-start.4 = (f32[1,64,256]{2,1,0:T(8,128)S(1)}, f32[1,64,256]{2,1,0:T(8,128)}, u32[]{:S(2)}) copy-start(f32[1,64,256]{2,1,0:T(8,128)} %param.9) | copy-start | bytes 196612
  5.0 0.7 copy-start.5
  74.5 3.4 %copy-start = (bf16[4,16,256,256]{3,2,1,0:T(8,128)(2,1)S(1)}, bf16[4,16,256,256]{3,2,1,0:T(8,128)(2,1)}, u32[]{:S(2)}) copy-start(bf16[4,16,256,256]{3,2,1,0:T(8,128)(2,1)} %layer.1.taken) | copy-start | bytes 25165828
